TPU v7x, 32 devices: a whole 2x2x4 slice. The times are simulated.
32 devices in a mesh: dp: 4 (over y, core), expert: 8 (over z, x).
Axes of the slice: x: 2, y: 2, z: 4, core: 2. Of those that a mesh axis runs over, the one named last changes fastest.
Arguments:
- tokens: bfloat16 [1024, 2560], P('expert'), may hold values from -6 to 6
- routes: int32 [1024, 6], P('expert'), may hold values from 0 to 7, as said below
- gate_probs: float32 [1024, 6], P('expert'), may hold values from 0.1 to 1
- shadow: int32 [1], replicated, may hold values from 0 to 7, as said below
- w_gate: bfloat16 [8, 1536, 2560], P('expert', 'dp'), may hold values from -0.125 to 0.125
- w_up: bfloat16 [8, 1536, 2560], P('expert', 'dp'), may hold values from -0.125 to 0.125
- w_down: bfloat16 [8, 1536, 2560], P('expert', 'dp'), may hold values from -0.15625 to 0.15625
- cotangent: bfloat16 [1024, 2560], P('expert'), may hold values from -6 to 6
Outputs:
- layer_out: bfloat16 [1024, 2560], P('expert', 'dp')
- grad_tokens: bfloat16 [1024, 2560], P('expert', 'dp')
- grad_gate: bfloat16 [8, 1536, 2560], P('expert', 'dp')
- grad_up: bfloat16 [8, 1536, 2560], P('expert', 'dp')
- grad_down: bfloat16 [8, 1536, 2560], P('expert', 'dp')
Inputs may be any that keep to these rules, and one draw needn't show every extreme that they name: `routes`: each row names 6 different experts. `shadow`: an expert id.
All inputs are finite; a program needn't handle non-finite values.
Results may differ from a plain program's by a relative error of at most 0.012.
Values may be sent and summed in bfloat16 or wider, within the bound.
A program may use at most 192 MiB of HBM per device.

v0:
```python
import jax
import jax.numpy as jnp
from jax import lax
from jax.sharding import PartitionSpec as P

TOP = 6


def spread(value, axis, source):
    kept = jnp.where(lax.axis_index(axis) == source, value, 0).astype(value.dtype)
    return lax.psum(kept, axis)


def rounded(numbers):
    return lax.optimization_barrier(numbers.astype(jnp.bfloat16))


def expert_rows(rows_x, rows_c, gate_w, up_w, down_w):
    contract = (((1,), (1,)), ((), ()))
    hidden = lax.dot_general(rows_x, gate_w, contract, preferred_element_type=jnp.float32)
    up_value = lax.dot_general(rows_x, up_w, contract, preferred_element_type=jnp.float32)
    gate_sigmoid = jax.nn.sigmoid(hidden)
    gated_hidden = hidden * gate_sigmoid
    active = (gated_hidden * up_value).astype(jnp.bfloat16)
    back_hidden = lax.dot_general(rows_c, down_w, contract, preferred_element_type=jnp.float32)
    d_hidden = (
        back_hidden * up_value * gate_sigmoid * (1.0 + hidden * (1.0 - gate_sigmoid))
    ).astype(jnp.bfloat16)
    d_up = (back_hidden * gated_hidden).astype(jnp.bfloat16)
    return (active, d_hidden, d_up)


def outer_sums(active, d_hidden, d_up, rows_x, rows_c):
    over_rows = (((0,), (0,)), ((), ()))
    return (
        lax.dot_general(d_hidden, rows_x, over_rows, preferred_element_type=jnp.float32),
        lax.dot_general(d_up, rows_x, over_rows, preferred_element_type=jnp.float32),
        lax.dot_general(active, rows_c, over_rows, preferred_element_type=jnp.float32),
    )


def expert_terms(active, d_hidden, d_up, gate_w, up_w, down_w):
    outputs = jnp.dot(active, down_w, preferred_element_type=jnp.float32)
    back_rows = jnp.dot(d_hidden, gate_w, preferred_element_type=jnp.float32)
    back_rows = back_rows + jnp.dot(d_up, up_w, preferred_element_type=jnp.float32)
    return jnp.stack([outputs, back_rows], axis=1)


def route_tables(routes, gate_probs, target, n_exp, capacity):
    token_count, route_count = routes.shape
    flattened = routes.reshape(-1)
    prob_flat = gate_probs.reshape(-1)
    onehot = (flattened[:, None] == lax.broadcasted_iota(jnp.int32, (1, n_exp), 1)).astype(
        jnp.int32
    )
    earlier = jnp.sum((jnp.cumsum(onehot, axis=0) - onehot) * onehot, axis=1)
    shadowed = flattened == target
    kept_pair = jnp.logical_and(jnp.logical_not(shadowed), earlier < capacity)
    dest_slot = flattened * capacity + earlier
    slot_iota = lax.broadcasted_iota(jnp.int32, (n_exp * capacity, 1), 0)
    chosen = jnp.logical_and(dest_slot[None, :] == slot_iota, kept_pair[None, :]).astype(
        jnp.float32
    )
    pick_tokens = jnp.sum(chosen.reshape(n_exp * capacity, token_count, route_count), axis=2)
    slot_prob = jnp.sum(chosen * prob_flat[None, :], axis=1)
    shadow_share = jnp.sum(
        jnp.where(shadowed, prob_flat, 0.0).reshape(token_count, route_count), axis=1
    )
    pair_slot = jnp.where(kept_pair, dest_slot, 0).reshape(token_count, route_count)
    pair_weight = jnp.where(kept_pair, prob_flat, 0.0).reshape(token_count, route_count)
    return (pick_tokens, slot_prob, shadow_share, pair_slot, pair_weight)


def body(tokens, routes, gate_probs, shadow, w_gate, w_up, w_down, cotangent):
    n_exp = lax.axis_size("expert")
    token_count, model_width = tokens.shape
    capacity = max(2, token_count * TOP // n_exp)
    slot_count = n_exp * capacity
    target = shadow[0]
    pick_tokens, slot_prob, shadow_share, pair_slot, pair_weight = route_tables(
        routes, gate_probs, target, n_exp, capacity
    )
    pick_narrow = pick_tokens.astype(jnp.bfloat16)
    send_x = jnp.dot(pick_narrow, tokens, preferred_element_type=jnp.float32)
    send_x = send_x.astype(jnp.bfloat16).reshape(n_exp, capacity, model_width)
    picked_cot = jnp.dot(pick_narrow, cotangent, preferred_element_type=jnp.float32)
    send_c = (
        (slot_prob[:, None] * picked_cot).astype(jnp.bfloat16).reshape(n_exp, capacity, model_width)
    )
    shadow_c = (shadow_share[:, None] * cotangent.astype(jnp.float32)).astype(jnp.bfloat16)
    copies = (
        spread(w_gate, "expert", target),
        spread(w_up, "expert", target),
        spread(w_down, "expert", target),
    )
    gate_s, up_s, down_s = (copies[0][0], copies[1][0], copies[2][0])
    gate_own, up_own, down_own = (w_gate[0], w_up[0], w_down[0])
    recv_x, recv_c = (
        lax.all_to_all(send_x, "expert", split_axis=0, concat_axis=0, tiled=True),
        lax.all_to_all(send_c, "expert", split_axis=0, concat_axis=0, tiled=True),
    )
    rows_x = recv_x.reshape(-1, model_width)
    rows_c = recv_c.reshape(-1, model_width)
    active, d_hidden, d_up = expert_rows(rows_x, rows_c, gate_own, up_own, down_own)
    partial_value = expert_terms(active, d_hidden, d_up, gate_own, up_own, down_own).astype(
        jnp.bfloat16
    )
    partial_value = partial_value.reshape(n_exp, capacity, 2, model_width)
    shadow_active, shadow_dh, shadow_du = expert_rows(tokens, shadow_c, gate_s, up_s, down_s)
    shadow_part = expert_terms(shadow_active, shadow_dh, shadow_du, gate_s, up_s, down_s).astype(
        jnp.bfloat16
    )
    shadow_part = shadow_part.reshape(token_count, 1, 2, model_width).astype(jnp.float32)
    returned = lax.all_to_all(partial_value, "expert", split_axis=0, concat_axis=0, tiled=True)
    summed, shadow_sum = (
        lax.psum_scatter(
            returned.astype(jnp.float32).astype(jnp.bfloat16), "dp", scatter_dimension=3, tiled=True
        ).astype(jnp.float32),
        lax.psum_scatter(
            shadow_part.astype(jnp.bfloat16), "dp", scatter_dimension=3, tiled=True
        ).astype(jnp.float32),
    )
    arrived = rounded(summed)
    arrived = arrived.reshape(slot_count, 2, -1)
    shadow_rows = rounded(shadow_sum).reshape(token_count, 2, -1)
    own_grads = outer_sums(active, d_hidden, d_up, rows_x, rows_c)
    shadow_parts = outer_sums(shadow_active, shadow_dh, shadow_du, tokens, shadow_c)
    shadow_grads = (
        lax.psum(shadow_parts[0].astype(jnp.bfloat16), "expert").astype(jnp.float32),
        lax.psum(shadow_parts[1].astype(jnp.bfloat16), "expert").astype(jnp.float32),
        lax.psum(shadow_parts[2].astype(jnp.bfloat16), "expert").astype(jnp.float32),
    )
    owner = lax.axis_index("expert") == target
    grad_gate = jnp.where(owner, shadow_grads[0], own_grads[0]).astype(jnp.bfloat16)[None]
    grad_up = jnp.where(owner, shadow_grads[1], own_grads[1]).astype(jnp.bfloat16)[None]
    grad_down = jnp.where(owner, shadow_grads[2], own_grads[2]).astype(jnp.bfloat16)[None]
    over_slots = (((0,), (0,)), ((), ()))
    out_rows = arrived[:, 0]
    back_rows = arrived[:, 1]
    feature_count = out_rows.shape[1]
    gathered_out = out_rows[pair_slot.reshape(-1)].reshape(token_count, TOP, feature_count)
    mixed_sum = jnp.sum(pair_weight[:, :, None] * gathered_out.astype(jnp.float32), axis=1)
    back_sum = lax.dot_general(
        pick_narrow, back_rows, over_slots, preferred_element_type=jnp.float32
    )
    layer_out = (mixed_sum + shadow_share[:, None] * shadow_rows[:, 0].astype(jnp.float32)).astype(
        jnp.bfloat16
    )
    grad_tokens = (back_sum + shadow_rows[:, 1].astype(jnp.float32)).astype(jnp.bfloat16)
    return (layer_out, grad_tokens, grad_gate, grad_up, grad_down)


def solution(mesh):
    placed = (
        P("expert", None),
        P("expert", None),
        P("expert", None),
        P(),
        P("expert", "dp", None),
        P("expert", "dp", None),
        P("expert", "dp", None),
        P("expert", None),
    )
    return jax.shard_map(
        body,
        mesh=mesh,
        in_specs=placed,
        out_specs=(
            P("expert", "dp"),
            P("expert", "dp"),
            P("expert", "dp", None),
            P("expert", "dp", None),
            P("expert", "dp", None),
        ),
        check_vma=False,
    )
```

profile of v0, /device:TPU:0, one launch (start us, length us, event | category | flops | bytes accessed | tf_op | source)
XLA Modules:
  0.0 882.2 jit_solution(11397315538269597978)
XLA Ops:
  14.8 3.0 multiply_convert_fusion
  17.9 7.3 all-to-all-start.1
  25.1 3.0 convolution_convert_fusion
  28.2 84.6 %all-to-all-done.1 = bf16[8,96,2560]{2,1,0:T(8,128)(2,1)} async-done(((bf16[8,96,2560]{2,1,0:T(8,128)(2,1)}), bf16[8,96,2560]{2,1,0:T(8,128)(2,1)}, u32[]{:S(2)}, u32[]{:S(2)}) %all-to-all-start.1) | async-done | bytes 3932192 | tf_op jit(solution)/shard_map/all_to_all | solution.py:100
  112.8 4.5 all-to-all-start
  117.6 3.1 select_bitcast_fusion
  120.7 2.2 select_bitcast_fusion.1
  122.9 6.0 fusion.13
  128.9 138.8 %all-to-all-done = bf16[8,96,2560]{2,1,0:T(8,128)(2,1)} async-done(((bf16[8,96,2560]{2,1,0:T(8,128)(2,1)}), bf16[8,96,2560]{2,1,0:T(8,128)(2,1)}, u32[]{:S(2)}, u32[]{:S(2)}) %all-to-all-start) | async-done | bytes 3932192 | tf_op jit(solution)/shard_map/all_to_all | solution.py:99
  267.7 4.5 fusion.20
  272.2 4.8 multiply_convert_fusion.4
  277.1 4.1 fusion
  281.1 2.2 fusion.18
  283.3 4.1 add_convert_fusion
  287.4 4.0 pad_maximum_fusion
  291.4 3.6 copy.54
  295.0 4.9 all-to-all-start.2
  300.2 242.2 %all-reduce.7.cloned.1.call-done = (bf16[384,2560]{1,0:T(8,128)(2,1)}, bf16[384,2560]{1,0:T(8,128)(2,1)}, bf16[384,2560]{1,0:T(8,128)(2,1)}) async-done(((bf16[384,2560]{1,0:T(8,128)(2,1)}, bf16[384,2560]{1,0:T(8,128)(2,1)}, bf16[384,2560]{1,0:T(8,128)(2,1)}), (bf16[384,2560]{1,0:T(8,128)(2,1)}, bf16[384,2560]{1,0:T(8,128)(2,1)}, bf16[384,2560]{1,0:T(8,128)(2,1)})) %all-reduce.7.cloned.1.call-update) | async-done | bytes 5898256 | tf_op jit(solution)/shard_map/psum | solution.py:11
  542.4 2.3 convolution_bitcast_fusion.1
  549.9 2.7 copy.62
  552.6 2.6 copy.67
  561.2 14.2 %copy.60 = bf16[8,96,2,2560]{1,0,2,3:T(8,128)(2,1)} copy(bf16[8,96,2,2560]{3,1,2,0:T(8,128)(2,1)} %all-to-all-done.2) | data formatting | bytes 15728640
  575.4 18.1 %reshape.219 = bf16[2560,1536]{1,0:T(8,128)(2,1)} reshape(bf16[2560,2,8,96]{3,2,1,0:T(8,128)(2,1)} %bitcast.123) | data formatting | bytes 15728640
  597.3 189.2 %all-reduce.5.cloned.1.call-done = (bf16[384,2560]{1,0:T(8,128)(2,1)}, bf16[384,2560]{1,0:T(8,128)(2,1)}, bf16[384,2560]{1,0:T(8,128)(2,1)}) async-done(((bf16[384,2560]{1,0:T(8,128)(2,1)}, bf16[384,2560]{1,0:T(8,128)(2,1)}, bf16[384,2560]{1,0:T(8,128)(2,1)}), (bf16[384,2560]{1,0:T(8,128)(2,1)}, bf16[384,2560]{1,0:T(8,128)(2,1)}, bf16[384,2560]{1,0:T(8,128)(2,1)})) %all-reduce.5.cloned.1.call-update) | async-done | bytes 5898256 | tf_op jit(solution)/shard_map/psum | solution.py:129
  786.5 5.9 fusion.4
  792.4 6.5 fusion.5
  798.9 5.7 fusion.6
  804.7 52.4 %reduce-scatter.7.cloned.1.call-done = bf16[640,1536]{1,0:T(8,128)(2,1)} async-done(((bf16[2560,1536]{1,0:T(8,128)(2,1)}), bf16[640,1536]{1,0:T(8,128)(2,1)}) %reduce-scatter.7.cloned.1.call-update) | async-done | bytes 1966096
  857.0 4.3 reshape.220
  861.3 3.4 copy.61
  868.5 3.4 gather_fusion
  871.9 2.0 reshape.207
  (116 shorter events, 27.7 us)
Async XLA Ops:
  7.2 18.0 %copy-start = (bf16[128,2560]{1,0:T(8,128)(2,1)S(1)}, bf16[128,2560]{1,0:T(8,128)(2,1)}, u32[]{:S(2)}) copy-start(bf16[128,2560]{1,0:T(8,128)(2,1)} %param.8) | copy-start | bytes 1966084
  7.2 7.6 copy-start.7
  10.6 3.2 copy-start.26
  17.9 94.9 %all-to-all-start.1 = ((bf16[8,96,2560]{2,1,0:T(8,128)(2,1)}), bf16[8,96,2560]{2,1,0:T(8,128)(2,1)}, u32[]{:S(2)}, u32[]{:S(2)}) async-start(bf16[8,96,2560]{2,1,0:T(8,128)(2,1)} %bitcast.125), calls=%async_computation.1 | async-start | bytes 7864320 | tf_op jit(solution)/shard_map/all_to_all | solution.py:100
  112.8 154.9 %all-to-all-start = ((bf16[8,96,2560]{2,1,0:T(8,128)(2,1)}), bf16[8,96,2560]{2,1,0:T(8,128)(2,1)}, u32[]{:S(2)}, u32[]{:S(2)}) async-start(bf16[8,96,2560]{2,1,0:T(8,128)(2,1)} %bitcast.124), calls=%async_computation | async-start | bytes 7864320 | tf_op jit(solution)/shard_map/all_to_all | solution.py:99
  117.3 425.1 %all-reduce.7.cloned.1.call-start = ((), (), s32[]{:S(2)}) async-start(), calls=%async_computation.8 | async-start | bytes 11796480 | tf_op jit(solution)/shard_map/psum | solution.py:11
  117.6 3.1 copy-start.1
  117.6 3.1 copy-start.2
  267.7 4.5 copy-start.3
  267.7 4.5 copy-start.31
  272.2 4.8 copy-start.14
  277.0 4.1 copy-start.17
  277.0 4.1 copy-start.10
  277.1 6.3 copy-start.8
  295.0 266.2 %all-to-all-start.2 = ((bf16[8,96,2,2560]{3,1,2,0:T(8,128)(2,1)}), bf16[8,96,2,2560]{3,1,2,0:T(8,128)(2,1)}, u32[]{:S(2)}, u32[]{:S(2)}) async-start(bf16[8,96,2,2560]{3,1,2,0:T(8,128)(2,1)} %copy.54), calls=%async_computation.2 | async-start | bytes 15728640 | tf_op jit(solution)/shard_map/all_to_all | solution.py:114
  299.9 244.9 %copy-start.28 = (f32[128]{0:T(128)S(1)}, f32[128]{0:T(128)}, u32[]{:S(2)}) copy-start(f32[128]{0:T(128)} %get-tuple-element.11) | copy-start | bytes 1540
  299.9 294.8 %reduce-scatter.9.cloned.1.call-start = ((), (), s32[]{:S(2)}) async-start(), calls=%async_computation.6 | async-start | bytes 1638400
  542.4 2.4 copy-start.5
  547.0 2.2 copy-start.19
  547.0 2.2 copy-start.21
  547.0 2.2 copy-start.23
  552.6 2.7 copy-start.24
  555.2 2.0 copy-start.22
  555.2 231.3 %all-reduce.5.cloned.1.call-start = ((), (), s32[]{:S(2)}) async-start(), calls=%async_computation.7 | async-start | bytes 11796480 | tf_op jit(solution)/shard_map/psum | solution.py:129
  557.2 1.9 copy-start.20
  557.2 1.9 copy-start.29
  561.2 295.9 %reduce-scatter.7.cloned.1.call-start = ((), (), s32[]{:S(2)}) async-start(), calls=%async_computation.5 | async-start | bytes 9830400
  593.5 193.0 %copy-start.18 = (bf16[768,384]{1,0:T(8,128)(2,1)S(1)}, bf16[768,384]{1,0:T(8,128)(2,1)}, u32[]{:S(2)}) copy-start(bf16[768,384]{1,0:T(8,128)(2,1)} %copy-done.17) | copy-start | bytes 1769476
  786.5 5.9 copy-start.9
  786.5 5.9 copy-start.13
  792.4 6.5 copy-start.11
  792.4 6.5 copy-start.12
  (7 other events, 8.9 us)
Sparse Core Ops, SparseCore 0:
  123.0 419.3 all-reduce.6
  555.3 24.3 reduce-scatter.8
  584.2 202.3 all-reduce.4
  789.1 67.9 reduce-scatter.6
where the time goes:
time: 884 us; the launch traced here: 882 us
  waiting for transfers between devices  707 us (80%)
  local copies, waits for them, and re-layouts  64.4 us (7%)
  matrix products  62.9 us (7%)
  starting transfers between devices  17.3 us (2%)
  other arithmetic  15.3 us (2%)
  between operations  14.9 us (2%)
    psum x1, waiting for transfers between devices, spread(): return lax.psum(kept, axis)  242 us
    psum x1, waiting for transfers between devices, body(): lax.psum(shadow_parts[0].astype(jnp.bfloat16), 'expert').astype(jnp.float32)  189 us
    all_to_all x1, waiting for transfers between devices, body(): lax.all_to_all(send_x, 'expert', split_axis=0, concat_axis=0, tiled=True)  139 us
    all_to_all x1, waiting for transfers between devices, body(): lax.all_to_all(send_c, 'expert', split_axis=0, concat_axis=0, tiled=True)  84.6 us
    unnamed x74, local copies, waits for them, and re-layouts  52.8 us
    unnamed x6, waiting for transfers between devices  52.5 us
  transfers between devices with their start and end apart: 7, of which 5 were waited for; matrix products, arithmetic and copies ran while one was open for 13% of the time, Pallas kernels for 0%

commit v1 on v0

v1 whole, which is shorter than its diff:
```python
import jax
import jax.numpy as jnp
from jax import lax
from jax.sharding import PartitionSpec as P

F32 = jnp.float32
BF16 = jnp.bfloat16
BOTH = ("expert", "dp")


def route_weights(routes, gate_probs, target, n_exp):
    token_count, top = routes.shape
    capacity = max(2, token_count * top // n_exp)
    experts = lax.broadcasted_iota(jnp.int32, (1, 1, n_exp), 2)
    match = routes[:, :, None] == experts
    prob = jnp.sum(jnp.where(match, gate_probs[:, :, None], 0.0), axis=1)
    hit = jnp.any(match, axis=1)
    row = lax.broadcasted_iota(jnp.int32, (token_count, token_count), 0)
    col = lax.broadcasted_iota(jnp.int32, (token_count, token_count), 1)
    earlier = jnp.dot((col < row).astype(BF16), hit.astype(BF16), preferred_element_type=F32)
    open_slot = jnp.logical_or(experts[0] == target, earlier < capacity)
    return jnp.where(jnp.logical_and(hit, open_slot), prob, 0.0)


def body(tokens, routes, gate_probs, shadow, w_gate, w_up, w_down, cotangent):
    n_exp = lax.axis_size("expert")
    n_dp = lax.axis_size("dp")
    token_count, width = tokens.shape
    part = token_count // n_dp
    dp = lax.axis_index("dp")
    expert = lax.axis_index("expert")
    weights = route_weights(routes, gate_probs, shadow[0], n_exp)
    mine = jnp.stack(
        [
            lax.dynamic_slice_in_dim(tokens, dp * part, part, 0),
            lax.dynamic_slice_in_dim(cotangent, dp * part, part, 0),
        ]
    )
    all_w = lax.all_gather(weights, "expert", axis=0, tiled=True)
    w = lax.dynamic_slice_in_dim(all_w, expert, 1, 1)
    both = lax.all_gather(mine, BOTH, axis=1, tiled=True)
    x = both[0]
    c = (w * both[1].astype(F32)).astype(BF16)
    gate_w, up_w, down_w = w_gate[0], w_up[0], w_down[0]
    contract = (((1,), (1,)), ((), ()))
    hidden = lax.dot_general(x, gate_w, contract, preferred_element_type=F32)
    up = lax.dot_general(x, up_w, contract, preferred_element_type=F32)
    back = lax.dot_general(c, down_w, contract, preferred_element_type=F32)
    sig = jax.nn.sigmoid(hidden)
    gated = hidden * sig
    active = (gated * up).astype(BF16)
    d_hidden = (back * up * sig * (1.0 + hidden * (1.0 - sig))).astype(BF16)
    d_up = (back * gated).astype(BF16)
    out = (w * jnp.dot(active, down_w, preferred_element_type=F32)).astype(BF16)
    back_rows = (
        jnp.dot(d_hidden, gate_w, preferred_element_type=F32)
        + jnp.dot(d_up, up_w, preferred_element_type=F32)
    ).astype(BF16)

    def chunks(value):
        value = value.reshape(n_exp, token_count, n_dp, width // n_dp)
        return value.transpose(0, 2, 1, 3)

    partial = jnp.stack([chunks(out), chunks(back_rows)], axis=2)
    partial = partial.reshape(n_exp * n_dp * 2 * token_count, width // n_dp)
    summed = lax.psum_scatter(partial, BOTH, scatter_dimension=0, tiled=True)
    over_rows = (((0,), (0,)), ((), ()))
    grads = [
        lax.dot_general(left, right, over_rows, preferred_element_type=F32).astype(BF16)[None]
        for left, right in ((d_hidden, x), (d_up, x), (active, c))
    ]
    summed = summed.reshape(2, token_count, width // n_dp)
    return (summed[0], summed[1], *grads)


def solution(mesh):
    rows = P("expert", None)
    split = P("expert", "dp", None)
    return jax.shard_map(
        body,
        mesh=mesh,
        in_specs=(rows, rows, rows, P(), split, split, split, rows),
        out_specs=(P("expert", "dp"), P("expert", "dp"), split, split, split),
        check_vma=False,
    )
```

time: 884 us -> 330 us (0.37)
  waiting for transfers between devices: 707 us -> 192 us
  blocking collectives: 0 us -> 32.6 us
  local copies, waits for them, and re-layouts: 64.4 us -> 34.7 us
  matrix products: 62.9 us -> 41.8 us
  starting transfers between devices: 17.3 us -> 0.08 us
    psum x2 -> x0, waiting for transfers between devices: 431 us -> none  [the longest x1 242 us: spread(): return lax.psum(kept, axis)]
    all_to_all x3 -> x0, waiting for transfers between devices: 223 us -> none  [the longest x1 139 us: body(): lax.all_to_all(send_x, 'expert', split_axis=0, concat_axis=0, tiled=True)]
    reduce_scatter x0 -> x1, waiting for transfers between devices: none -> 135 us  [body(): summed = lax.psum_scatter(partial, BOTH, scatter_dimension=0, tiled=True)]
    all_gather x0 -> x1, waiting for transfers between devices: none -> 56.9 us  [body(): both = lax.all_gather(mine, BOTH, axis=1, tiled=True)]
    unnamed x6 -> x2, waiting for transfers between devices: 52.5 us -> 0.03 us
    unnamed x74 -> x18, local copies, waits for them, and re-layouts: 52.8 us -> 1.98 us
    all_gather x0 -> x1, blocking collectives: none -> 32.6 us  [body(): all_w = lax.all_gather(weights, 'expert', axis=0, tiled=True)]
    dot_general x21 -> x10, matrix products: 62.9 us -> 41.8 us  [the longest x3 16 us: body(): lax.dot_general(left, right, over_rows, preferred_element_type=F32)]
  transfers between devices with their start and end apart: 7 -> 2, of which waited for: 5 -> 2; matrix products, arithmetic and copies ran while one was open for 13% -> 5% of each run, Pallas kernels for 0% -> 0%
where the time goes in v1:
time: 330 us; the launch traced here: 329 us
  waiting for transfers between devices  192 us (58%)
  matrix products  41.8 us (13%)
  local copies, waits for them, and re-layouts  34.7 us (11%)
  blocking collectives  32.6 us (10%)
  between operations  14.8 us (4%)
  other arithmetic  12.5 us (4%)
    reduce_scatter x1, waiting for transfers between devices, body(): summed = lax.psum_scatter(partial, BOTH, scatter_dimension=0, tiled=True)  135 us
    all_gather x1, waiting for transfers between devices, body(): both = lax.all_gather(mine, BOTH, axis=1, tiled=True)  56.9 us
    all_gather x1, blocking collectives, body(): all_w = lax.all_gather(weights, 'expert', axis=0, tiled=True)  32.6 us
    reshape x2, local copies, waits for them, and re-layouts, chunks(): value = value.reshape(n_exp, token_count, n_dp, width // n_dp)  19.6 us
    dot_general x3, matrix products, body(): lax.dot_general(left, right, over_rows, preferred_element_type=F32)  16 us
    another operation x1, other arithmetic, body(): partial = jnp.stack([chunks(out), chunks(back_rows)], axis=2)  10.3 us
    another operation x1, local copies, waits for them, and re-layouts, body(): partial = jnp.stack([chunks(out), chunks(back_rows)], axis=2)  10.2 us
  transfers between devices with their start and end apart: 2, of which 2 were waited for; matrix products, arithmetic and copies ran while one was open for 5% of the time, Pallas kernels for 0%

profile of v1, /device:TPU:0, one launch (start us, length us, event | category | flops | bytes accessed | tf_op | source)
XLA Modules:
  0.0 328.6 jit_solution(3645577066294977002)
XLA Ops:
  7.2 0.0 copy-start
  7.2 0.0 all-gather.2.cloned.1.call-start
  7.2 1.2 dynamic-slice_bitcast_fusion
  8.4 0.8 pad_maximum_fusion.1
  9.1 0.0 all-gather.2.cloned.1.call-update
  9.2 0.0 reduce-scatter.2.cloned.1.call-start
  9.9 0.7 fusion.33
  10.6 0.7 select_reduce_fusion
  11.3 0.1 fusion.32
  11.4 32.6 %all_gather.6 = f32[1024,8]{0,1:T(8,128)S(1)} all-gather(f32[128,8]{0,1:T(8,128)S(1)} %fusion.32), channel_id=1, replica_groups=mesh['dp'=4,'expert'=8] {'expert'}, dimensions={0}, use_global_device_ids=true | all-gather | bytes 36864 | tf_op jit(solution)/shard_map/all_gather | solution.py:39
  44.0 56.9 %all-gather.2.cloned.1.call-done = bf16[2,1024,2560]{2,1,0:T(8,128)(2,1)} async-done(((bf16[2,32,2560]{2,1,0:T(8,128)(2,1)}), bf16[2,1024,2560]{2,1,0:T(8,128)(2,1)}) %all-gather.2.cloned.1.call-update) | async-done | bytes 10485776 | tf_op jit(solution)/shard_map/all_gather | solution.py:41
  100.8 5.6 %fusion.21 = f32[1024,384]{1,0:T(8,128)S(1)} fusion(bf16[2,1024,2560]{2,1,0:T(8,128)(2,1)} %all-gather.2.cloned.1.call-done, bf16[1,384,2560]{2,1,0:T(8,128)(2,1)} %param.12), kind=kOutput, calls=%fused_computation.23 | convolution fusion | flops 2013265920 | bytes 8781824 | tf_op jit(solution)/shard_map/dot_general | solution.py:46
  106.4 0.5 copy-done.2
  106.9 0.5 copy-done.3
  107.5 2.9 fusion.6
  110.4 3.4 %multiply_convert_fusion.3 = (bf16[1024,384]{1,0:T(8,128)(2,1)S(1)}, bf16[1024,384]{1,0:T(8,128)(2,1)S(1)}, bf16[1024,384]{1,0:T(8,128)(2,1)S(1)}) fusion(f32[1024,384]{1,0:T(8,128)S(1)} %fusion.21, f32[1024,384]{1,0:T(8,128)S(1)} %fusion.6, bf16[1,384,2560]{2,1,0:T(8,128)(2,1)S(1)} %copy-done, bf16[2,1024,2560]{2,1,0:T(8,128)(2,1)S(1)} %copy-done.2), kind=kOutput, calls=%fused_computation.33 | convolution fusion | flops 2019164160 | bytes 12713984 | tf_op jit(solution)/shard_map/dot_general | solution.py:47
  113.8 0.0 copy-start.4
  113.8 0.9 copy-done.4
  114.7 4.6 %multiply_convert_fusion = bf16[1024,2560]{1,0:T(8,128)(2,1)} fusion(bf16[1024,384]{1,0:T(8,128)(2,1)S(1)} %get-tuple-element.5, f32[1024]{0:T(1024)S(1)} %bitcast.70, bf16[1,384,2560]{2,1,0:T(8,128)(2,1)S(1)} %copy-done.3), kind=kOutput, calls=%fused_computation.7 | convolution fusion | flops 2018508800 | bytes 7999488 | tf_op jit(solution)/shard_map/dot_general | solution.py:54
  119.3 9.8 %reshape.41 = bf16[8,128,4,640]{3,2,1,0:T(4,128)(2,1)} reshape(bf16[1024,2560]{1,0:T(8,128)(2,1)} %multiply_convert_fusion) | data formatting | bytes 10485760 | tf_op jit(solution)/shard_map/reshape | solution.py:61
  129.1 4.4 %fusion.26 = f32[1024,2560]{1,0:T(8,128)S(1)} fusion(bf16[1024,384]{1,0:T(8,128)(2,1)S(1)} %get-tuple-element.6, bf16[1,384,2560]{2,1,0:T(8,128)(2,1)} %param.12), kind=kOutput, calls=%fused_computation.28 | convolution fusion | flops 2013265920 | bytes 13238272 | tf_op jit(solution)/shard_map/dot_general | solution.py:56
  133.6 4.7 %add_convert_fusion = bf16[1024,2560]{1,0:T(8,128)(2,1)} fusion(f32[1024,2560]{1,0:T(8,128)S(1)} %fusion.26, bf16[1024,384]{1,0:T(8,128)(2,1)S(1)} %get-tuple-element.7, bf16[1,384,2560]{2,1,0:T(8,128)(2,1)S(1)} %copy-done), kind=kOutput, calls=%fused_computation.6 | convolution fusion | flops 2018508800 | bytes 18481152 | tf_op jit(solution)/shard_map/dot_general | solution.py:57
  138.2 9.8 %reshape.42 = bf16[8,128,4,640]{3,2,1,0:T(4,128)(2,1)} reshape(bf16[1024,2560]{1,0:T(8,128)(2,1)} %add_convert_fusion) | data formatting | bytes 10485760 | tf_op jit(solution)/shard_map/reshape | solution.py:61
  148.0 10.3 %pad_maximum_fusion = bf16[8,4,2,128,640]{4,1,3,0,2:T(4,128)(2,1)} fusion(bf16[8,4,1,128,640]{4,1,3,0,2:T(4,128)(2,1)} %bitcast.68, bf16[8,4,1,128,640]{4,1,3,0,2:T(4,128)(2,1)} %bitcast.67), kind=kLoop, calls=%fused_computation.5 | loop fusion | flops 5242880 | bytes 20971520 | tf_op jit(solution)/shard_map/stack | solution.py:64
  158.3 10.2 %copy.16 = bf16[8,4,2,128,640]{4,3,2,1,0:T(8,128)(2,1)} copy(bf16[8,4,2,128,640]{4,1,3,0,2:T(4,128)(2,1)} %pad_maximum_fusion) | data formatting | bytes 20971520 | tf_op jit(solution)/shard_map/stack | solution.py:64
  168.6 0.0 reduce-scatter.2.cloned.1.call-update
  168.6 0.0 slice-start.1
  168.6 6.1 %fusion.15 = bf16[1,384,2560]{2,1,0:T(8,128)(2,1)} fusion(bf16[1024,384]{1,0:T(8,128)(2,1)S(1)} %get-tuple-element.6, bf16[2,1024,2560]{2,1,0:T(8,128)(2,1)} %all-gather.2.cloned.1.call-done), kind=kOutput, calls=%fused_computation.19 | convolution fusion | flops 2014248960 | bytes 7995392 | tf_op jit(solution)/shard_map/dot_general | solution.py:69
  174.8 6.1 %fusion.16 = bf16[1,384,2560]{2,1,0:T(8,128)(2,1)} fusion(bf16[1024,384]{1,0:T(8,128)(2,1)S(1)} %get-tuple-element.7, bf16[2,1024,2560]{2,1,0:T(8,128)(2,1)} %all-gather.2.cloned.1.call-done), kind=kOutput, calls=%fused_computation.20 | convolution fusion | flops 2014248960 | bytes 7995392 | tf_op jit(solution)/shard_map/dot_general | solution.py:69
  180.9 3.8 %fusion.17 = bf16[1,384,2560]{2,1,0:T(8,128)(2,1)} fusion(bf16[1024,384]{1,0:T(8,128)(2,1)S(1)} %copy-done.5, f32[1024]{0:T(1024)S(1)} %bitcast.71, bf16[2,1024,2560]{2,1,0:T(8,128)(2,1)S(1)} %bitcast.73), kind=kOutput, calls=%fused_computation.21 | convolution fusion | flops 2022113280 | bytes 7999488 | tf_op jit(solution)/shard_map/dot_general | solution.py:69
  184.7 135.4 %reduce-scatter.2.cloned.1.call-done = bf16[256,640]{1,0:T(8,128)(2,1)} async-done(((bf16[8192,640]{1,0:T(8,128)(2,1)}), bf16[256,640]{1,0:T(8,128)(2,1)}) %reduce-scatter.2.cloned.1.call-update) | async-done | bytes 327696 | tf_op jit(solution)/shard_map/reduce_scatter | solution.py:66
  320.1 1.7 fusion.34
  (15 shorter events, 0.0 us)
Async XLA Ops:
  7.2 103.2 %copy-start = (bf16[1,384,2560]{2,1,0:T(8,128)(2,1)S(1)}, bf16[1,384,2560]{2,1,0:T(8,128)(2,1)}, u32[]{:S(2)}) copy-start(bf16[1,384,2560]{2,1,0:T(8,128)(2,1)} %param.13) | copy-start | bytes 5898244
  7.2 93.6 %all-gather.2.cloned.1.call-start = ((), (), s32[]{:S(2)}) async-start(), calls=%async_computation.1 | async-start | bytes 10813440 | tf_op jit(solution)/shard_map/all_gather | solution.py:41
  9.2 310.9 %reduce-scatter.2.cloned.1.call-start = ((), (), s32[]{:S(2)}) async-start(), calls=%async_computation.2 | async-start | bytes 10813440 | tf_op jit(solution)/shard_map/reduce_scatter | solution.py:66
  100.8 6.1 %copy-start.2 = (bf16[2,1024,2560]{2,1,0:T(8,128)(2,1)S(1)}, bf16[2,1024,2560]{2,1,0:T(8,128)(2,1)}, u32[]{:S(2)}) copy-start(bf16[2,1024,2560]{2,1,0:T(8,128)(2,1)} %all-gather.2.cloned.1.call-done) | copy-start | bytes 31457284
  100.8 6.7 %copy-start.3 = (bf16[1,384,2560]{2,1,0:T(8,128)(2,1)S(1)}, bf16[1,384,2560]{2,1,0:T(8,128)(2,1)}, u32[]{:S(2)}) copy-start(bf16[1,384,2560]{2,1,0:T(8,128)(2,1)} %param.14) | copy-start | bytes 5898244
  113.8 0.9 copy-start.4
  168.6 12.3 %slice-start = ((s8[10485760]{0:T(1024)(128)(4,1)}), s8[4194304]{0:T(1024)(128)(4,1)S(1)}, s32[]{:S(2)}) async-start(s8[10485760]{0:T(1024)(128)(4,1)} %bitcast.72), calls=%async_computation.3 | async-start | bytes 8388608
  168.6 12.3 %slice-start.1 = ((s8[10485760]{0:T(1024)(128)(4,1)}), s8[4194304]{0:T(1024)(128)(4,1)S(1)}, s32[]{:S(2)}) async-start(s8[10485760]{0:T(1024)(128)(4,1)} %bitcast.72), calls=%async_computation.4 | async-start | bytes 8388608
  174.8 6.2 %slice-start.2 = ((s8[10485760]{0:T(1024)(128)(4,1)}), s8[2097152]{0:T(1024)(128)(4,1)S(1)}, s32[]{:S(2)}) async-start(s8[10485760]{0:T(1024)(128)(4,1)} %bitcast.72), calls=%async_computation.5 | async-start | bytes 4194304
  174.8 6.2 %copy-start.5 = (bf16[1024,384]{1,0:T(8,128)(2,1)S(1)}, bf16[1024,384]{1,0:T(8,128)(2,1)}, u32[]{:S(2)}) copy-start(bf16[1024,384]{1,0:T(8,128)(2,1)} %copy-done.4) | copy-start | bytes 2359300
  174.8 147.0 %copy-start.1 = (bf16[1,384,2560]{2,1,0:T(8,128)(2,1)S(1)}, bf16[1,384,2560]{2,1,0:T(8,128)(2,1)}, u32[]{:S(2)}) copy-start(bf16[1,384,2560]{2,1,0:T(8,128)(2,1)} %param.13) | copy-start | bytes 5898244
Sparse Core Ops, SparseCore 0:
  11.5 89.2 all-gather.1
  168.7 151.2 reduce-scatter.1

commit v2 on v1

--- a/solution.py
+++ b/solution.py
@@ -20,6 +20,43 @@
     earlier = jnp.dot((col < row).astype(BF16), hit.astype(BF16), preferred_element_type=F32)
     open_slot = jnp.logical_or(experts[0] == target, earlier < capacity)
     return jnp.where(jnp.logical_and(hit, open_slot), prob, 0.0)
+
+
+def swap(value, axis, bit):
+    size = lax.axis_size(axis)
+    return lax.ppermute(value, axis, [(i, i ^ (1 << bit)) for i in range(size)])
+
+
+def add(left, right):
+    return (left.astype(F32) + right.astype(F32)).astype(BF16)
+
+
+def halve(parts, stages, ex_bits):
+    left = list(range(ex_bits - 1, -1, -1))
+    for axis, bit in stages:
+        if axis == "dp":
+            mask = 1 << bit
+            parts = {
+                j: add(value, swap(parts[j ^ mask], axis, bit))
+                for j, value in parts.items()
+                if not j & mask
+            }
+        else:
+            place = left.index(bit)
+            left.remove(bit)
+            mine = (lax.axis_index(axis) >> bit) % 2
+            parts = {
+                j: add(
+                    lax.dynamic_index_in_dim(value, mine, place, keepdims=False),
+                    swap(
+                        lax.dynamic_index_in_dim(value, 1 - mine, place, keepdims=False),
+                        axis,
+                        bit,
+                    ),
+                )
+                for j, value in parts.items()
+            }
+    return parts[0]
 
 
 def body(tokens, routes, gate_probs, shadow, w_gate, w_up, w_down, cotangent):
@@ -51,26 +88,29 @@
     active = (gated * up).astype(BF16)
     d_hidden = (back * up * sig * (1.0 + hidden * (1.0 - sig))).astype(BF16)
     d_up = (back * gated).astype(BF16)
-    out = (w * jnp.dot(active, down_w, preferred_element_type=F32)).astype(BF16)
-    back_rows = (
-        jnp.dot(d_hidden, gate_w, preferred_element_type=F32)
-        + jnp.dot(d_up, up_w, preferred_element_type=F32)
-    ).astype(BF16)
-
-    def chunks(value):
-        value = value.reshape(n_exp, token_count, n_dp, width // n_dp)
-        return value.transpose(0, 2, 1, 3)
-
-    partial = jnp.stack([chunks(out), chunks(back_rows)], axis=2)
-    partial = partial.reshape(n_exp * n_dp * 2 * token_count, width // n_dp)
-    summed = lax.psum_scatter(partial, BOTH, scatter_dimension=0, tiled=True)
+    cols = width // n_dp
+    dp_bits, ex_bits = n_dp.bit_length() - 1, n_exp.bit_length() - 1
+    blocks = (2,) * ex_bits + (token_count, cols)
+    out_parts, back_parts = {}, {}
+    order = sorted(range(n_dp), key=lambda j: (1 - j % 2, j))
+    for j in order:
+        start = jnp.bitwise_xor(dp, j) * cols
+        cut = [lax.dynamic_slice_in_dim(m, start, cols, 1) for m in (gate_w, up_w, down_w)]
+        value = w * jnp.dot(active, cut[2], preferred_element_type=F32)
+        out_parts[j] = value.astype(BF16).reshape(blocks)
+        value = jnp.dot(d_hidden, cut[0], preferred_element_type=F32)
+        value = value + jnp.dot(d_up, cut[1], preferred_element_type=F32)
+        back_parts[j] = value.astype(BF16).reshape(blocks)
+    rest_dp = [("dp", b) for b in range(1, dp_bits)]
+    rest_ex = [("expert", b) for b in range(1, ex_bits)]
+    layer_out = halve(out_parts, [("dp", 0), *rest_dp, ("expert", 0), *rest_ex], ex_bits)
+    grad_tokens = halve(back_parts, [("dp", 0), ("expert", 0), *rest_dp, *rest_ex], ex_bits)
     over_rows = (((0,), (0,)), ((), ()))
     grads = [
         lax.dot_general(left, right, over_rows, preferred_element_type=F32).astype(BF16)[None]
         for left, right in ((d_hidden, x), (d_up, x), (active, c))
     ]
-    summed = summed.reshape(2, token_count, width // n_dp)
-    return (summed[0], summed[1], *grads)
+    return (layer_out, grad_tokens, *grads)
 
 
 def solution(mesh):

time: 330 us -> 216 us (0.65)
  waiting for transfers between devices: 192 us -> 112 us
  local copies, waits for them, and re-layouts: 34.7 us -> 3.71 us
  starting transfers between devices: 0.08 us -> 11.8 us
  matrix products: 41.8 us -> 34.1 us
  other arithmetic: 12.5 us -> 5.92 us
    reduce_scatter x1 -> x0, waiting for transfers between devices: 135 us -> none  [body(): summed = lax.psum_scatter(partial, BOTH, scatter_dimension=0, tiled=True)]
    ppermute x0 -> x13, waiting for transfers between devices: none -> 55.2 us  [swap(): return lax.ppermute(value, axis, [(i, i ^ 1 << bit) for i in range(size)])]
    reshape x2 -> x4, local copies, waits for them, and re-layouts: 19.6 us -> 0.48 us  [the longest x2 0.25 us: body(): out_parts[j] = value.astype(BF16).reshape(blocks)]
    ppermute x0 -> x13, starting transfers between devices: none -> 11.8 us  [swap(): return lax.ppermute(value, axis, [(i, i ^ 1 << bit) for i in range(size)])]
    another operation x1 -> x0, other arithmetic: 10.3 us -> none  [body(): partial = jnp.stack([chunks(out), chunks(back_rows)], axis=2)]
    another operation x1 -> x0, local copies, waits for them, and re-layouts: 10.2 us -> none  [body(): partial = jnp.stack([chunks(out), chunks(back_rows)], axis=2)]
    dot_general x3, matrix products: 16 us -> 11.1 us  [body(): lax.dot_general(left, right, over_rows, preferred_element_type=F32)]
    convert_element_type x0 -> x11, other arithmetic: none -> 3.75 us  [add(): return (left.astype(F32) + right.astype(F32)).astype(BF16)]
  transfers between devices with their start and end apart: 2 -> 14, of which waited for: 2 -> 8; matrix products, arithmetic and copies ran while one was open for 5% -> 11% of each run, Pallas kernels for 0% -> 0%
where the time goes in v2:
time: 216 us; the launch traced here: 215 us
  waiting for transfers between devices  112 us (52%)
  matrix products  34.1 us (16%)
  blocking collectives  32.5 us (15%)
  between operations  15.1 us (7%)
  starting transfers between devices  11.8 us (5%)
  other arithmetic  5.92 us (3%)
  local copies, waits for them, and re-layouts  3.71 us (2%)
    all_gather x1, waiting for transfers between devices, body(): both = lax.all_gather(mine, BOTH, axis=1, tiled=True)  56.8 us
    ppermute x13, waiting for transfers between devices, swap(): return lax.ppermute(value, axis, [(i, i ^ 1 << bit) for i in range(size)])  55.2 us
    all_gather x1, blocking collectives, body(): all_w = lax.all_gather(weights, 'expert', axis=0, tiled=True)  32.5 us
    ppermute x13, starting transfers between devices, swap(): return lax.ppermute(value, axis, [(i, i ^ 1 << bit) for i in range(size)])  11.8 us
    dot_general x3, matrix products, body(): lax.dot_general(left, right, over_rows, preferred_element_type=F32)  11.1 us
    dot_general x1, matrix products, body(): up = lax.dot_general(x, up_w, contract, preferred_element_type=F32)  5.57 us
  transfers between devices with their start and end apart: 14, of which 8 were waited for; matrix products, arithmetic and copies ran while one was open for 11% of the time, Pallas kernels for 0%

profile of v2, /device:TPU:0, one launch (start us, length us, event | category | flops | bytes accessed | tf_op | source)
XLA Modules:
  0.0 215.3 jit_solution(10260831887528683794)
XLA Ops:
  7.2 1.2 dynamic-slice_bitcast_fusion.7
  11.4 32.5 %all_gather.6 = f32[1024,8]{0,1:T(8,128)S(1)} all-gather(f32[128,8]{0,1:T(8,128)S(1)} %fusion.35), channel_id=1, replica_groups=mesh['dp'=4,'expert'=8] {'expert'}, dimensions={0}, use_global_device_ids=true | all-gather | bytes 36864 | tf_op jit(solution)/shard_map/all_gather | solution.py:76
  44.0 56.8 %all-gather.2.cloned.1.call-done = bf16[2,1024,2560]{2,1,0:T(8,128)(2,1)} async-done(((bf16[2,32,2560]{2,1,0:T(8,128)(2,1)}), bf16[2,1024,2560]{2,1,0:T(8,128)(2,1)}) %all-gather.2.cloned.1.call-update) | async-done | bytes 10485776 | tf_op jit(solution)/shard_map/all_gather | solution.py:78
  100.8 5.6 %fusion.20 = f32[1024,384]{1,0:T(8,128)S(1)} fusion(bf16[2,1024,2560]{2,1,0:T(8,128)(2,1)} %all-gather.2.cloned.1.call-done, bf16[1,384,2560]{2,1,0:T(8,128)(2,1)} %param.13), kind=kOutput, calls=%fused_computation.19 | convolution fusion | flops 2013265920 | bytes 8781824 | tf_op jit(solution)/shard_map/dot_general | solution.py:84
  106.4 1.1 copy-done.3
  107.5 2.9 %fusion.21 = f32[1024,384]{1,0:T(8,128)S(1)} fusion(bf16[2,1024,2560]{2,1,0:T(8,128)(2,1)S(1)} %copy-done.3, bf16[1,384,2560]{2,1,0:T(8,128)(2,1)S(1)} %copy-done.1), kind=kOutput, calls=%fused_computation.20 | convolution fusion | flops 2013265920 | bytes 8781824 | tf_op jit(solution)/shard_map/dot_general | solution.py:83
  110.4 3.5 %multiply_convert_fusion.4 = (bf16[1024,384]{1,0:T(8,128)(2,1)S(1)}, bf16[1024,384]{1,0:T(8,128)(2,1)S(1)}, bf16[1024,384]{1,0:T(8,128)(2,1)S(1)}) fusion(f32[1024,384]{1,0:T(8,128)S(1)} %fusion.21, f32[1024,384]{1,0:T(8,128)S(1)} %fusion.20, bf16[1,384,2560]{2,1,0:T(8,128)(2,1)S(1)} %copy-done, f32[1024]{0:T(1024)S(1)} %bitcast.153, ...), kind=kOutput, calls=%fused_computation.41 | convolution fusion | flops 2027028480 | bytes 12718080 | tf_op jit(solution)/shard_map/dot_general | solution.py:85
  114.0 0.9 fusion.39
  114.9 0.9 fusion.45
  115.8 0.9 multiply_convert_fusion
  116.7 0.9 multiply_convert_fusion.2
  119.6 0.9 add_convert_fusion.2
  121.9 0.9 add_convert_fusion.3
  123.8 3.7 %fusion.15 = bf16[1,384,2560]{2,1,0:T(8,128)(2,1)} fusion(bf16[1024,384]{1,0:T(8,128)(2,1)S(1)} %get-tuple-element.6, bf16[2,1024,2560]{2,1,0:T(8,128)(2,1)S(1)} %copy-done.3), kind=kOutput, calls=%fused_computation.16 | convolution fusion | flops 2014248960 | bytes 7995392 | tf_op jit(solution)/shard_map/dot_general | solution.py:110
  128.4 0.9 add_convert_fusion.1
  129.3 3.8 %fusion.17 = bf16[1,384,2560]{2,1,0:T(8,128)(2,1)} fusion(bf16[1024,384]{1,0:T(8,128)(2,1)S(1)} %get-tuple-element.7, f32[1024]{0:T(1024)S(1)} %bitcast.156, bf16[2,1024,2560]{2,1,0:T(8,128)(2,1)S(1)} %copy-done.3), kind=kOutput, calls=%fused_computation.18 | convolution fusion | flops 2022113280 | bytes 7999488 | tf_op jit(solution)/shard_map/dot_general | solution.py:110
  133.2 0.9 multiply_convert_fusion.1
  134.5 1.6 collective-permute-start.2
  137.1 0.9 multiply_convert_fusion.3
  138.4 1.5 collective-permute-start.7
  139.9 14.2 %collective-permute-done.9 = bf16[2,2,128,640]{3,2,0,1:T(8,128)(2,1)S(1)} collective-permute-done((bf16[2,2,128,640]{3,2,0,1:T(8,128)(2,1)S(1)}, bf16[2,2,128,640]{3,2,0,1:T(8,128)(2,1)S(1)}, u32[]{:S(2)}, u32[]{:S(2)}) %collective-permute-start.9) | collective-permute-done | bytes 655392 | tf_op jit(solution)/shard_map/ppermute | solution.py:27
  154.9 11.2 %collective-permute-done.2 = bf16[2,2,2,128,640]{4,3,0,1,2:T(8,128)(2,1)S(1)} collective-permute-done((bf16[2,2,2,128,640]{4,3,0,1,2:T(8,128)(2,1)S(1)}, bf16[2,2,2,128,640]{4,3,0,1,2:T(8,128)(2,1)S(1)}, u32[]{:S(2)}, u32[]{:S(2)}) %collective-permute-start.2) | collective-permute-done | bytes 1310752 | tf_op jit(solution)/shard_map/ppermute | solution.py:27
  166.7 1.5 collective-permute-start.3
  168.2 3.5 %fusion.16 = bf16[1,384,2560]{2,1,0:T(8,128)(2,1)} fusion(bf16[1024,384]{1,0:T(8,128)(2,1)S(1)} %get-tuple-element.5, bf16[2,1024,2560]{2,1,0:T(8,128)(2,1)S(1)} %copy-done.3), kind=kOutput, calls=%fused_computation.17 | convolution fusion | flops 2014248960 | bytes 7995392 | tf_op jit(solution)/shard_map/dot_general | solution.py:110
  171.7 7.8 %collective-permute-done.10 = bf16[2,2,128,640]{3,2,0,1:T(8,128)(2,1)S(1)} collective-permute-done((bf16[2,2,128,640]{3,2,0,1:T(8,128)(2,1)S(1)}, bf16[2,2,128,640]{3,2,0,1:T(8,128)(2,1)S(1)}, u32[]{:S(2)}, u32[]{:S(2)}) %collective-permute-start.10) | collective-permute-done | bytes 655392 | tf_op jit(solution)/shard_map/ppermute | solution.py:27
  179.8 1.4 collective-permute-start.11
  181.2 1.0 collective-permute-done.3
  182.5 1.4 collective-permute-start.4
  183.8 6.7 %collective-permute-done.11 = bf16[2,128,640]{2,1,0:T(8,128)(2,1)S(1)} collective-permute-done((bf16[2,128,640]{2,1,0:T(8,128)(2,1)S(1)}, bf16[2,128,640]{2,1,0:T(8,128)(2,1)S(1)}, u32[]{:S(2)}, u32[]{:S(2)}) %collective-permute-start.11) | collective-permute-done | bytes 327712 | tf_op jit(solution)/shard_map/ppermute | solution.py:27
  190.6 1.9 collective-permute-start.12
  192.5 6.9 %collective-permute-done.4 = bf16[2,128,640]{2,1,0:T(8,128)(2,1)S(1)} collective-permute-done((bf16[2,128,640]{2,1,0:T(8,128)(2,1)S(1)}, bf16[2,128,640]{2,1,0:T(8,128)(2,1)S(1)}, u32[]{:S(2)}, u32[]{:S(2)}) %collective-permute-start.4) | collective-permute-done | bytes 327712 | tf_op jit(solution)/shard_map/ppermute | solution.py:27
  200.4 7.3 %collective-permute-done.5 = bf16[128,640]{1,0:T(8,128)(2,1)S(1)} collective-permute-done((bf16[128,640]{1,0:T(8,128)(2,1)S(1)}, bf16[128,640]{1,0:T(8,128)(2,1)S(1)}, u32[]{:S(2)}, u32[]{:S(2)}) %collective-permute-start.5) | collective-permute-done | bytes 163872 | tf_op jit(solution)/shard_map/ppermute | solution.py:27
  (53 shorter events, 12.8 us)
Async XLA Ops:
  7.2 103.2 %copy-start = (bf16[1,384,2560]{2,1,0:T(8,128)(2,1)S(1)}, bf16[1,384,2560]{2,1,0:T(8,128)(2,1)}, u32[]{:S(2)}) copy-start(bf16[1,384,2560]{2,1,0:T(8,128)(2,1)} %param.14) | copy-start | bytes 5898244
  7.2 93.6 %all-gather.2.cloned.1.call-start = ((), (), s32[]{:S(2)}) async-start(), calls=%async_computation | async-start | bytes 10813440 | tf_op jit(solution)/shard_map/all_gather | solution.py:78
  100.8 5.6 %copy-start.1 = (bf16[1,384,2560]{2,1,0:T(8,128)(2,1)S(1)}, bf16[1,384,2560]{2,1,0:T(8,128)(2,1)}, u32[]{:S(2)}) copy-start(bf16[1,384,2560]{2,1,0:T(8,128)(2,1)} %param.12) | copy-start | bytes 5898244
  100.8 6.7 %copy-start.3 = (bf16[2,1024,2560]{2,1,0:T(8,128)(2,1)S(1)}, bf16[2,1024,2560]{2,1,0:T(8,128)(2,1)}, u32[]{:S(2)}) copy-start(bf16[2,1024,2560]{2,1,0:T(8,128)(2,1)} %all-gather.2.cloned.1.call-done) | copy-start | bytes 31457284
  116.7 1.5 copy-start.2
  119.3 16.7 %collective-permute-start.8 = (bf16[2,2,2,128,640]{4,3,0,1,2:T(8,128)(2,1)S(1)}, bf16[2,2,2,128,640]{4,3,0,1,2:T(8,128)(2,1)S(1)}, u32[]{:S(2)}, u32[]{:S(2)}) collective-permute-start(bf16[2,2,2,128,640]{4,3,0,1,2:T(8,128)(2,1)S(1)} %copy.29), channel_id=1, source_target_pairs={{0,8},{8,0},{16,24},{24,16},{1,9},{9,1},{17,25},{25,17},{2,10},{10... | collective-permute-start | bytes 3932168 | tf_op jit(solution)/shard_map/ppermute | solution.py:27
  120.7 17.3 %collective-permute-start.6 = (bf16[2,2,2,128,640]{4,3,0,1,2:T(8,128)(2,1)S(1)}, bf16[2,2,2,128,640]{4,3,0,1,2:T(8,128)(2,1)S(1)}, u32[]{:S(2)}, u32[]{:S(2)}) collective-permute-start(bf16[2,2,2,128,640]{4,3,0,1,2:T(8,128)(2,1)S(1)} %copy.27), channel_id=1, source_target_pairs={{0,8},{8,0},{16,24},{24,16},{1,9},{9,1},{17,25},{25,17},{2,10},{10... | collective-permute-start | bytes 3932168 | tf_op jit(solution)/shard_map/ppermute | solution.py:27
  123.0 11.1 %collective-permute-start.1 = (bf16[2,2,2,128,640]{4,3,0,1,2:T(8,128)(2,1)S(1)}, bf16[2,2,2,128,640]{4,3,0,1,2:T(8,128)(2,1)S(1)}, u32[]{:S(2)}, u32[]{:S(2)}) collective-permute-start(bf16[2,2,2,128,640]{4,3,0,1,2:T(8,128)(2,1)S(1)} %copy.25), channel_id=1, source_target_pairs={{0,8},{8,0},{16,24},{24,16},{1,9},{9,1},{17,25},{25,17},{2,10},{10... | collective-permute-start | bytes 3932168 | tf_op jit(solution)/shard_map/ppermute | solution.py:27
  123.5 31.4 %collective-permute-start = (bf16[2,2,2,128,640]{4,3,0,1,2:T(8,128)(2,1)S(1)}, bf16[2,2,2,128,640]{4,3,0,1,2:T(8,128)(2,1)S(1)}, u32[]{:S(2)}, u32[]{:S(2)}) collective-permute-start(bf16[2,2,2,128,640]{4,3,0,1,2:T(8,128)(2,1)S(1)} %copy.23), channel_id=1, source_target_pairs={{0,8},{8,0},{16,24},{24,16},{1,9},{9,1},{17,25},{25,17},{2,10},{10... | collective-permute-start | bytes 3932168 | tf_op jit(solution)/shard_map/ppermute | solution.py:27
  134.5 31.7 %collective-permute-start.2 = (bf16[2,2,2,128,640]{4,3,0,1,2:T(8,128)(2,1)S(1)}, bf16[2,2,2,128,640]{4,3,0,1,2:T(8,128)(2,1)S(1)}, u32[]{:S(2)}, u32[]{:S(2)}) collective-permute-start(bf16[2,2,2,128,640]{4,3,0,1,2:T(8,128)(2,1)S(1)} %fusion.24), channel_id=1, source_target_pairs={{0,16},{8,24},{16,0},{24,8},{1,17},{9,25},{17,1},{25,9},{2,18},{10... | collective-permute-start | bytes 3932168 | tf_op jit(solution)/shard_map/ppermute | solution.py:27
  136.4 17.7 %collective-permute-start.9 = (bf16[2,2,128,640]{3,2,0,1:T(8,128)(2,1)S(1)}, bf16[2,2,128,640]{3,2,0,1:T(8,128)(2,1)S(1)}, u32[]{:S(2)}, u32[]{:S(2)}) collective-permute-start(bf16[2,2,128,640]{3,2,0,1:T(8,128)(2,1)S(1)} %dynamic-slice_bitcast_fusion), channel_id=1, source_target_pairs={{0,1},{1,0},{2,3},{3,2},{4,5},{5,4},{6,7},{7,6},{8,9},{9,8},{10,11... | collective-permute-start | bytes 1966088 | tf_op jit(solution)/shard_map/ppermute | solution.py:27
  138.4 33.3 %collective-permute-start.7 = (bf16[2,2,128,640]{3,2,0,1:T(8,128)(2,1)S(1)}, bf16[2,2,128,640]{3,2,0,1:T(8,128)(2,1)S(1)}, u32[]{:S(2)}, u32[]{:S(2)}) collective-permute-start(bf16[2,2,128,640]{3,2,0,1:T(8,128)(2,1)S(1)} %dynamic-slice_bitcast_fusion.1), channel_id=1, source_target_pairs={{0,1},{1,0},{2,3},{3,2},{4,5},{5,4},{6,7},{7,6},{8,9},{9,8},{10,11... | collective-permute-start | bytes 1966088 | tf_op jit(solution)/shard_map/ppermute | solution.py:27
  154.3 25.2 %collective-permute-start.10 = (bf16[2,2,128,640]{3,2,0,1:T(8,128)(2,1)S(1)}, bf16[2,2,128,640]{3,2,0,1:T(8,128)(2,1)S(1)}, u32[]{:S(2)}, u32[]{:S(2)}) collective-permute-start(bf16[2,2,128,640]{3,2,0,1:T(8,128)(2,1)S(1)} %fusion.30), channel_id=1, source_target_pairs={{0,16},{8,24},{16,0},{24,8},{1,17},{9,25},{17,1},{25,9},{2,18},{10... | collective-permute-start | bytes 1966088 | tf_op jit(solution)/shard_map/ppermute | solution.py:27
  166.7 15.5 %collective-permute-start.3 = (bf16[2,2,128,640]{3,2,0,1:T(8,128)(2,1)S(1)}, bf16[2,2,128,640]{3,2,0,1:T(8,128)(2,1)S(1)}, u32[]{:S(2)}, u32[]{:S(2)}) collective-permute-start(bf16[2,2,128,640]{3,2,0,1:T(8,128)(2,1)S(1)} %dynamic-slice_bitcast_fusion.2), channel_id=1, source_target_pairs={{0,1},{1,0},{2,3},{3,2},{4,5},{5,4},{6,7},{7,6},{8,9},{9,8},{10,11... | collective-permute-start | bytes 1966088 | tf_op jit(solution)/shard_map/ppermute | solution.py:27
  179.8 10.7 %collective-permute-start.11 = (bf16[2,128,640]{2,1,0:T(8,128)(2,1)S(1)}, bf16[2,128,640]{2,1,0:T(8,128)(2,1)S(1)}, u32[]{:S(2)}, u32[]{:S(2)}) collective-permute-start(bf16[2,128,640]{2,1,0:T(8,128)(2,1)S(1)} %dynamic-slice_bitcast_fusion.3), channel_id=1, source_target_pairs={{0,2},{1,3},{2,0},{3,1},{4,6},{5,7},{6,4},{7,5},{8,10},{9,11},{10,... | collective-permute-start | bytes 983048 | tf_op jit(solution)/shard_map/ppermute | solution.py:27
  182.5 17.0 %collective-permute-start.4 = (bf16[2,128,640]{2,1,0:T(8,128)(2,1)S(1)}, bf16[2,128,640]{2,1,0:T(8,128)(2,1)S(1)}, u32[]{:S(2)}, u32[]{:S(2)}) collective-permute-start(bf16[2,128,640]{2,1,0:T(8,128)(2,1)S(1)} %dynamic-slice_bitcast_fusion.4), channel_id=1, source_target_pairs={{0,2},{1,3},{2,0},{3,1},{4,6},{5,7},{6,4},{7,5},{8,10},{9,11},{10,... | collective-permute-start | bytes 983048 | tf_op jit(solution)/shard_map/ppermute | solution.py:27
  190.6 9.0 %collective-permute-start.12 = (bf16[128,640]{1,0:T(8,128)(2,1)S(1)}, bf16[128,640]{1,0:T(8,128)(2,1)S(1)}, u32[]{:S(2)}, u32[]{:S(2)}) collective-permute-start(bf16[128,640]{1,0:T(8,128)(2,1)S(1)} %dynamic-slice_bitcast_fusion.5), channel_id=1, source_target_pairs={{0,4},{1,5},{2,6},{3,7},{4,0},{5,1},{6,2},{7,3},{8,12},{9,13},{10,... | collective-permute-start | bytes 491528 | tf_op jit(solution)/shard_map/ppermute | solution.py:27
  199.6 8.2 %collective-permute-start.5 = (bf16[128,640]{1,0:T(8,128)(2,1)S(1)}, bf16[128,640]{1,0:T(8,128)(2,1)S(1)}, u32[]{:S(2)}, u32[]{:S(2)}) collective-permute-start(bf16[128,640]{1,0:T(8,128)(2,1)S(1)} %dynamic-slice_bitcast_fusion.6), channel_id=1, source_target_pairs={{0,4},{1,5},{2,6},{3,7},{4,0},{5,1},{6,2},{7,3},{8,12},{9,13},{10,... | collective-permute-start | bytes 491528 | tf_op jit(solution)/shard_map/ppermute | solution.py:27
Sparse Core Ops, SparseCore 0:
  11.5 89.2 all-gather.1

commit v3 on v2

--- a/solution.py
+++ b/solution.py
@@ -103,6 +103,9 @@
         back_parts[j] = value.astype(BF16).reshape(blocks)
     rest_dp = [("dp", b) for b in range(1, dp_bits)]
     rest_ex = [("expert", b) for b in range(1, ex_bits)]
+    d_hidden, d_up, active, out_parts[0], back_parts[0] = lax.optimization_barrier(
+        (d_hidden, d_up, active, out_parts[0], back_parts[0])
+    )
     layer_out = halve(out_parts, [("dp", 0), *rest_dp, ("expert", 0), *rest_ex], ex_bits)
     grad_tokens = halve(back_parts, [("dp", 0), ("expert", 0), *rest_dp, *rest_ex], ex_bits)
     over_rows = (((0,), (0,)), ((), ()))

time: 216 us -> 213 us (0.986)
    dot_general x1, matrix products: 2.88 us -> 5.57 us  [body(): hidden = lax.dot_general(x, gate_w, contract, preferred_element_type=F32)]
    dot_general x1, matrix products: 5.57 us -> 2.88 us  [body(): up = lax.dot_general(x, up_w, contract, preferred_element_type=F32)]
    ppermute x13, waiting for transfers between devices: 55.2 us -> 52.7 us  [swap(): return lax.ppermute(value, axis, [(i, i ^ 1 << bit) for i in range(size)])]
where the time goes in v3:
time: 213 us
  waiting for transfers between devices  110 us (52%)
  matrix products  34.2 us (16%)
  blocking collectives  32.5 us (15%)
  between operations  15.1 us (7%)
  starting transfers between devices  11.8 us (6%)
  other arithmetic  5.9 us (3%)
  local copies, waits for them, and re-layouts  3.74 us (2%)
    all_gather x1, waiting for transfers between devices, body(): both = lax.all_gather(mine, BOTH, axis=1, tiled=True)  56.8 us
    ppermute x13, waiting for transfers between devices, swap(): return lax.ppermute(value, axis, [(i, i ^ 1 << bit) for i in range(size)])  52.7 us
    all_gather x1, blocking collectives, body(): all_w = lax.all_gather(weights, 'expert', axis=0, tiled=True)  32.5 us
    ppermute x13, starting transfers between devices, swap(): return lax.ppermute(value, axis, [(i, i ^ 1 << bit) for i in range(size)])  11.8 us
    dot_general x3, matrix products, body(): lax.dot_general(left, right, over_rows, preferred_element_type=F32)  10.9 us
    dot_general x1, matrix products, body(): hidden = lax.dot_general(x, gate_w, contract, preferred_element_type=F32)  5.57 us
  transfers between devices with their start and end apart: 14, of which 8 were waited for; matrix products, arithmetic and copies ran while one was open for 11% of the time, Pallas kernels for 0%

profile of v3, /device:TPU:0, one launch (start us, length us, event | category | flops | bytes accessed | tf_op | source)
XLA Modules:
  0.0 212.8 jit_solution(11542295477518898999)
XLA Ops:
  7.2 1.2 dynamic-slice_bitcast_fusion.7
  11.4 32.5 %all_gather.6 = f32[1024,8]{0,1:T(8,128)S(1)} all-gather(f32[128,8]{0,1:T(8,128)S(1)} %fusion.33), channel_id=1, replica_groups=mesh['dp'=4,'expert'=8] {'expert'}, dimensions={0}, use_global_device_ids=true | all-gather | bytes 36864 | tf_op jit(solution)/shard_map/all_gather | solution.py:76
  44.0 56.8 %all-gather.2.cloned.1.call-done = bf16[2,1024,2560]{2,1,0:T(8,128)(2,1)} async-done(((bf16[2,32,2560]{2,1,0:T(8,128)(2,1)}), bf16[2,1024,2560]{2,1,0:T(8,128)(2,1)}) %all-gather.2.cloned.1.call-update) | async-done | bytes 10485776 | tf_op jit(solution)/shard_map/all_gather | solution.py:78
  100.8 5.6 %fusion.20 = f32[1024,384]{1,0:T(8,128)S(1)} fusion(bf16[2,1024,2560]{2,1,0:T(8,128)(2,1)} %all-gather.2.cloned.1.call-done, bf16[1,384,2560]{2,1,0:T(8,128)(2,1)} %param.12), kind=kOutput, calls=%fused_computation.19 | convolution fusion | flops 2013265920 | bytes 8781824 | tf_op jit(solution)/shard_map/dot_general | solution.py:83
  106.4 1.1 copy-done.3
  107.5 2.9 %fusion.21 = f32[1024,384]{1,0:T(8,128)S(1)} fusion(bf16[2,1024,2560]{2,1,0:T(8,128)(2,1)S(1)} %copy-done.3, bf16[1,384,2560]{2,1,0:T(8,128)(2,1)S(1)} %copy-done.2), kind=kOutput, calls=%fused_computation.20 | convolution fusion | flops 2013265920 | bytes 8781824 | tf_op jit(solution)/shard_map/dot_general | solution.py:84
  110.4 3.5 %multiply_convert_fusion.5 = (bf16[1024,384]{1,0:T(8,128)(2,1)S(1)}, bf16[1024,384]{1,0:T(8,128)(2,1)S(1)}, bf16[1024,384]{1,0:T(8,128)(2,1)S(1)}) fusion(f32[1024,384]{1,0:T(8,128)S(1)} %fusion.20, f32[1024,384]{1,0:T(8,128)S(1)} %fusion.21, bf16[1,384,2560]{2,1,0:T(8,128)(2,1)S(1)} %copy-done, f32[1024]{0:T(1024)S(1)} %bitcast.151, ...), kind=kOutput, calls=%fused_computation.40 | convolution fusion | flops 2027028480 | bytes 12718080 | tf_op jit(solution)/shard_map/dot_general | solution.py:85
  114.0 0.9 multiply_convert_fusion
  114.9 0.9 multiply_convert_fusion.2
  117.3 0.9 fusion.43
  120.1 0.9 add_convert_fusion.6
  121.0 0.9 add_convert_fusion
  123.4 1.1 add_convert_fusion.3
  124.5 0.9 multiply_convert_fusion.1
  125.4 0.9 multiply_convert_fusion.3
  126.8 0.9 add_convert_fusion.1
  127.7 3.8 %fusion.17 = bf16[1,384,2560]{2,1,0:T(8,128)(2,1)} fusion(bf16[1024,384]{1,0:T(8,128)(2,1)S(1)} %get-tuple-element.14, f32[1024]{0:T(1024)S(1)} %bitcast.156, bf16[2,1024,2560]{2,1,0:T(8,128)(2,1)S(1)} %copy-done.3), kind=kOutput, calls=%fused_computation.18 | convolution fusion | flops 2022113280 | bytes 7999488 | tf_op jit(solution)/shard_map/dot_general | solution.py:113
  131.9 1.5 collective-permute-start.2
  134.5 3.5 %fusion.15 = bf16[1,384,2560]{2,1,0:T(8,128)(2,1)} fusion(bf16[1024,384]{1,0:T(8,128)(2,1)S(1)} %get-tuple-element.12, bf16[2,1024,2560]{2,1,0:T(8,128)(2,1)S(1)} %copy-done.3), kind=kOutput, calls=%fused_computation.16 | convolution fusion | flops 2014248960 | bytes 7995392 | tf_op jit(solution)/shard_map/dot_general | solution.py:113
  138.5 1.5 collective-permute-start.7
  140.0 11.6 %collective-permute-done.9 = bf16[2,2,128,640]{3,2,0,1:T(8,128)(2,1)S(1)} collective-permute-done((bf16[2,2,128,640]{3,2,0,1:T(8,128)(2,1)S(1)}, bf16[2,2,128,640]{3,2,0,1:T(8,128)(2,1)S(1)}, u32[]{:S(2)}, u32[]{:S(2)}) %collective-permute-start.9) | collective-permute-done | bytes 655392 | tf_op jit(solution)/shard_map/ppermute | solution.py:27
  152.4 11.2 %collective-permute-done.2 = bf16[2,2,2,128,640]{4,3,0,1,2:T(8,128)(2,1)S(1)} collective-permute-done((bf16[2,2,2,128,640]{4,3,0,1,2:T(8,128)(2,1)S(1)}, bf16[2,2,2,128,640]{4,3,0,1,2:T(8,128)(2,1)S(1)}, u32[]{:S(2)}, u32[]{:S(2)}) %collective-permute-start.2) | collective-permute-done | bytes 1310752 | tf_op jit(solution)/shard_map/ppermute | solution.py:27
  164.2 1.5 collective-permute-start.3
  165.7 3.5 %fusion.16 = bf16[1,384,2560]{2,1,0:T(8,128)(2,1)} fusion(bf16[1024,384]{1,0:T(8,128)(2,1)S(1)} %get-tuple-element.13, bf16[2,1024,2560]{2,1,0:T(8,128)(2,1)S(1)} %copy-done.3), kind=kOutput, calls=%fused_computation.17 | convolution fusion | flops 2014248960 | bytes 7995392 | tf_op jit(solution)/shard_map/dot_general | solution.py:113
  169.2 7.8 %collective-permute-done.10 = bf16[2,2,128,640]{3,2,0,1:T(8,128)(2,1)S(1)} collective-permute-done((bf16[2,2,128,640]{3,2,0,1:T(8,128)(2,1)S(1)}, bf16[2,2,128,640]{3,2,0,1:T(8,128)(2,1)S(1)}, u32[]{:S(2)}, u32[]{:S(2)}) %collective-permute-start.10) | collective-permute-done | bytes 655392 | tf_op jit(solution)/shard_map/ppermute | solution.py:27
  177.3 1.4 collective-permute-start.11
  178.7 1.0 collective-permute-done.3
  179.9 1.4 collective-permute-start.4
  181.3 6.7 %collective-permute-done.11 = bf16[2,128,640]{2,1,0:T(8,128)(2,1)S(1)} collective-permute-done((bf16[2,128,640]{2,1,0:T(8,128)(2,1)S(1)}, bf16[2,128,640]{2,1,0:T(8,128)(2,1)S(1)}, u32[]{:S(2)}, u32[]{:S(2)}) %collective-permute-start.11) | collective-permute-done | bytes 327712 | tf_op jit(solution)/shard_map/ppermute | solution.py:27
  188.1 1.9 collective-permute-start.12
  190.0 7.0 %collective-permute-done.4 = bf16[2,128,640]{2,1,0:T(8,128)(2,1)S(1)} collective-permute-done((bf16[2,128,640]{2,1,0:T(8,128)(2,1)S(1)}, bf16[2,128,640]{2,1,0:T(8,128)(2,1)S(1)}, u32[]{:S(2)}, u32[]{:S(2)}) %collective-permute-start.4) | collective-permute-done | bytes 327712 | tf_op jit(solution)/shard_map/ppermute | solution.py:27
  197.9 7.4 %collective-permute-done.5 = bf16[128,640]{1,0:T(8,128)(2,1)S(1)} collective-permute-done((bf16[128,640]{1,0:T(8,128)(2,1)S(1)}, bf16[128,640]{1,0:T(8,128)(2,1)S(1)}, u32[]{:S(2)}, u32[]{:S(2)}) %collective-permute-start.5) | collective-permute-done | bytes 163872 | tf_op jit(solution)/shard_map/ppermute | solution.py:27
  (53 shorter events, 12.8 us)
Async XLA Ops:
  7.2 103.2 %copy-start = (bf16[1,384,2560]{2,1,0:T(8,128)(2,1)S(1)}, bf16[1,384,2560]{2,1,0:T(8,128)(2,1)}, u32[]{:S(2)}) copy-start(bf16[1,384,2560]{2,1,0:T(8,128)(2,1)} %param.14) | copy-start | bytes 5898244
  7.2 93.6 %all-gather.2.cloned.1.call-start = ((), (), s32[]{:S(2)}) async-start(), calls=%async_computation | async-start | bytes 10813440 | tf_op jit(solution)/shard_map/all_gather | solution.py:78
  100.8 5.6 %copy-start.2 = (bf16[1,384,2560]{2,1,0:T(8,128)(2,1)S(1)}, bf16[1,384,2560]{2,1,0:T(8,128)(2,1)}, u32[]{:S(2)}) copy-start(bf16[1,384,2560]{2,1,0:T(8,128)(2,1)} %param.13) | copy-start | bytes 5898244
  100.8 6.7 %copy-start.3 = (bf16[2,1024,2560]{2,1,0:T(8,128)(2,1)S(1)}, bf16[2,1024,2560]{2,1,0:T(8,128)(2,1)}, u32[]{:S(2)}) copy-start(bf16[2,1024,2560]{2,1,0:T(8,128)(2,1)} %all-gather.2.cloned.1.call-done) | copy-start | bytes 31457284
  114.9 1.5 copy-start.1
  118.4 13.2 %collective-permute-start.1 = (bf16[2,2,2,128,640]{4,3,0,1,2:T(8,128)(2,1)S(1)}, bf16[2,2,2,128,640]{4,3,0,1,2:T(8,128)(2,1)S(1)}, u32[]{:S(2)}, u32[]{:S(2)}) collective-permute-start(bf16[2,2,2,128,640]{4,3,0,1,2:T(8,128)(2,1)S(1)} %copy.25), channel_id=1, source_target_pairs={{0,8},{8,0},{16,24},{24,16},{1,9},{9,1},{17,25},{25,17},{2,10},{10... | collective-permute-start | bytes 3932168 | tf_op jit(solution)/shard_map/ppermute | solution.py:27
  118.9 33.5 %collective-permute-start = (bf16[2,2,2,128,640]{4,3,0,1,2:T(8,128)(2,1)S(1)}, bf16[2,2,2,128,640]{4,3,0,1,2:T(8,128)(2,1)S(1)}, u32[]{:S(2)}, u32[]{:S(2)}) collective-permute-start(bf16[2,2,2,128,640]{4,3,0,1,2:T(8,128)(2,1)S(1)} %copy.24), channel_id=1, source_target_pairs={{0,8},{8,0},{16,24},{24,16},{1,9},{9,1},{17,25},{25,17},{2,10},{10... | collective-permute-start | bytes 3932168 | tf_op jit(solution)/shard_map/ppermute | solution.py:27
  122.1 11.4 %collective-permute-start.8 = (bf16[2,2,2,128,640]{4,3,0,1,2:T(8,128)(2,1)S(1)}, bf16[2,2,2,128,640]{4,3,0,1,2:T(8,128)(2,1)S(1)}, u32[]{:S(2)}, u32[]{:S(2)}) collective-permute-start(bf16[2,2,2,128,640]{4,3,0,1,2:T(8,128)(2,1)S(1)} %copy.29), channel_id=1, source_target_pairs={{0,8},{8,0},{16,24},{24,16},{1,9},{9,1},{17,25},{25,17},{2,10},{10... | collective-permute-start | bytes 3932168 | tf_op jit(solution)/shard_map/ppermute | solution.py:27
  126.5 11.5 %collective-permute-start.6 = (bf16[2,2,2,128,640]{4,3,0,1,2:T(8,128)(2,1)S(1)}, bf16[2,2,2,128,640]{4,3,0,1,2:T(8,128)(2,1)S(1)}, u32[]{:S(2)}, u32[]{:S(2)}) collective-permute-start(bf16[2,2,2,128,640]{4,3,0,1,2:T(8,128)(2,1)S(1)} %copy.28), channel_id=1, source_target_pairs={{0,8},{8,0},{16,24},{24,16},{1,9},{9,1},{17,25},{25,17},{2,10},{10... | collective-permute-start | bytes 3932168 | tf_op jit(solution)/shard_map/ppermute | solution.py:27
  131.9 31.7 %collective-permute-start.2 = (bf16[2,2,2,128,640]{4,3,0,1,2:T(8,128)(2,1)S(1)}, bf16[2,2,2,128,640]{4,3,0,1,2:T(8,128)(2,1)S(1)}, u32[]{:S(2)}, u32[]{:S(2)}) collective-permute-start(bf16[2,2,2,128,640]{4,3,0,1,2:T(8,128)(2,1)S(1)} %fusion.23), channel_id=1, source_target_pairs={{0,16},{8,24},{16,0},{24,8},{1,17},{9,25},{17,1},{25,9},{2,18},{10... | collective-permute-start | bytes 3932168 | tf_op jit(solution)/shard_map/ppermute | solution.py:27
  133.9 17.7 %collective-permute-start.9 = (bf16[2,2,128,640]{3,2,0,1:T(8,128)(2,1)S(1)}, bf16[2,2,128,640]{3,2,0,1:T(8,128)(2,1)S(1)}, u32[]{:S(2)}, u32[]{:S(2)}) collective-permute-start(bf16[2,2,128,640]{3,2,0,1:T(8,128)(2,1)S(1)} %dynamic-slice_bitcast_fusion), channel_id=1, source_target_pairs={{0,1},{1,0},{2,3},{3,2},{4,5},{5,4},{6,7},{7,6},{8,9},{9,8},{10,11... | collective-permute-start | bytes 1966088 | tf_op jit(solution)/shard_map/ppermute | solution.py:27
  138.5 30.7 %collective-permute-start.7 = (bf16[2,2,128,640]{3,2,0,1:T(8,128)(2,1)S(1)}, bf16[2,2,128,640]{3,2,0,1:T(8,128)(2,1)S(1)}, u32[]{:S(2)}, u32[]{:S(2)}) collective-permute-start(bf16[2,2,128,640]{3,2,0,1:T(8,128)(2,1)S(1)} %dynamic-slice_bitcast_fusion.1), channel_id=1, source_target_pairs={{0,1},{1,0},{2,3},{3,2},{4,5},{5,4},{6,7},{7,6},{8,9},{9,8},{10,11... | collective-permute-start | bytes 1966088 | tf_op jit(solution)/shard_map/ppermute | solution.py:27
  151.7 25.3 %collective-permute-start.10 = (bf16[2,2,128,640]{3,2,0,1:T(8,128)(2,1)S(1)}, bf16[2,2,128,640]{3,2,0,1:T(8,128)(2,1)S(1)}, u32[]{:S(2)}, u32[]{:S(2)}) collective-permute-start(bf16[2,2,128,640]{3,2,0,1:T(8,128)(2,1)S(1)} %fusion.28), channel_id=1, source_target_pairs={{0,16},{8,24},{16,0},{24,8},{1,17},{9,25},{17,1},{25,9},{2,18},{10... | collective-permute-start | bytes 1966088 | tf_op jit(solution)/shard_map/ppermute | solution.py:27
  164.2 15.5 %collective-permute-start.3 = (bf16[2,2,128,640]{3,2,0,1:T(8,128)(2,1)S(1)}, bf16[2,2,128,640]{3,2,0,1:T(8,128)(2,1)S(1)}, u32[]{:S(2)}, u32[]{:S(2)}) collective-permute-start(bf16[2,2,128,640]{3,2,0,1:T(8,128)(2,1)S(1)} %dynamic-slice_bitcast_fusion.2), channel_id=1, source_target_pairs={{0,1},{1,0},{2,3},{3,2},{4,5},{5,4},{6,7},{7,6},{8,9},{9,8},{10,11... | collective-permute-start | bytes 1966088 | tf_op jit(solution)/shard_map/ppermute | solution.py:27
  177.3 10.7 %collective-permute-start.11 = (bf16[2,128,640]{2,1,0:T(8,128)(2,1)S(1)}, bf16[2,128,640]{2,1,0:T(8,128)(2,1)S(1)}, u32[]{:S(2)}, u32[]{:S(2)}) collective-permute-start(bf16[2,128,640]{2,1,0:T(8,128)(2,1)S(1)} %dynamic-slice_bitcast_fusion.3), channel_id=1, source_target_pairs={{0,2},{1,3},{2,0},{3,1},{4,6},{5,7},{6,4},{7,5},{8,10},{9,11},{10,... | collective-permute-start | bytes 983048 | tf_op jit(solution)/shard_map/ppermute | solution.py:27
  179.9 17.1 %collective-permute-start.4 = (bf16[2,128,640]{2,1,0:T(8,128)(2,1)S(1)}, bf16[2,128,640]{2,1,0:T(8,128)(2,1)S(1)}, u32[]{:S(2)}, u32[]{:S(2)}) collective-permute-start(bf16[2,128,640]{2,1,0:T(8,128)(2,1)S(1)} %dynamic-slice_bitcast_fusion.4), channel_id=1, source_target_pairs={{0,2},{1,3},{2,0},{3,1},{4,6},{5,7},{6,4},{7,5},{8,10},{9,11},{10,... | collective-permute-start | bytes 983048 | tf_op jit(solution)/shard_map/ppermute | solution.py:27
  188.1 9.0 %collective-permute-start.12 = (bf16[128,640]{1,0:T(8,128)(2,1)S(1)}, bf16[128,640]{1,0:T(8,128)(2,1)S(1)}, u32[]{:S(2)}, u32[]{:S(2)}) collective-permute-start(bf16[128,640]{1,0:T(8,128)(2,1)S(1)} %dynamic-slice_bitcast_fusion.5), channel_id=1, source_target_pairs={{0,4},{1,5},{2,6},{3,7},{4,0},{5,1},{6,2},{7,3},{8,12},{9,13},{10,... | collective-permute-start | bytes 491528 | tf_op jit(solution)/shard_map/ppermute | solution.py:27
  197.1 8.2 %collective-permute-start.5 = (bf16[128,640]{1,0:T(8,128)(2,1)S(1)}, bf16[128,640]{1,0:T(8,128)(2,1)S(1)}, u32[]{:S(2)}, u32[]{:S(2)}) collective-permute-start(bf16[128,640]{1,0:T(8,128)(2,1)S(1)} %dynamic-slice_bitcast_fusion.6), channel_id=1, source_target_pairs={{0,4},{1,5},{2,6},{3,7},{4,0},{5,1},{6,2},{7,3},{8,12},{9,13},{10,... | collective-permute-start | bytes 491528 | tf_op jit(solution)/shard_map/ppermute | solution.py:27
Sparse Core Ops, SparseCore 0:
  11.5 89.2 all-gather.1
